TPU v7x, 256 devices: a whole 4x4x8 slice. The times are simulated.
256 devices in a mesh: region: 16 (over y, x), block: 16 (over z, core).
Axes of the slice: x: 4, y: 4, z: 8, core: 2. Of those that a mesh axis runs over, the one named last changes fastest.
Arguments:
- gap_terms: float32 [16, 16, 1536, 128], P('region', 'block'), may hold values from -6 to 6
- rigid_loads: float32 [16, 16, 6, 128], P('region', 'block'), may hold values from -384 to 384
- dual_matrix: bfloat16 [16, 16, 1536, 1536], P('region', 'block'), as said below
- dirichlet_matrix: bfloat16 [16, 16, 1536, 1536], P('region', 'block'), as said below
- rigid_modes: float32 [16, 16, 6, 1536], P('region', 'block'), as said below
- coarse_rows: float32 [16, 16, 6, 1536], P('region', 'block'), as said below
- face_slot: int32 [16, 16, 4], P('region', 'block'), may hold values from 0 to 5, as said below
- glue_sign: int32 [16, 16, 1536], P('region', 'block'), may hold values from -1 to 1, as said below
Outputs:
- multiplier: float32 [16, 16, 1536, 128], P('region', 'block')
Inputs may be any that keep to these rules, and one draw needn't show every extreme that they name: `face_slot`: for each subdomain, four different slots; the two slots left hold multipliers of the clamped boundary. Row i of a face and row i of the facing face of the neighbour are one constraint. `glue_sign`: each entry is -1 or 1; a multiplier shared by two subdomains has opposite signs on its two sides. `rigid_modes`: on a face shared by two subdomains both hold the same values, row by row. `coarse_rows`: the rows of this subdomain's 6 modes in a symmetric positive definite coarse operator of order 1536, which stands in for the inverse of G^T G, where G maps c to the field that rigid assembles from signed_modes^T c. `dual_matrix`: symmetric positive definite. `dirichlet_matrix`: symmetric positive definite.
All inputs are finite; a program needn't handle non-finite values.
Results may differ from a plain program's by a relative error of at most 0.0026.
Values sent between devices are 32-bit elements; how exact they have to be, the bound alone decides.
A program may use at most 64 MiB of HBM per device.

v0:
```python
import jax
import jax.numpy as jnp
from jax import lax
from jax.sharding import PartitionSpec as P

FACE = 256
ITERS = 2


precise = lax.Precision.HIGHEST


def shifted(block, axis, distance):
    devices = range(lax.axis_size(axis))
    route = [(i - distance, i) for i in devices if i - distance in devices]
    return lax.ppermute(block, axis, route)


def face_rows(vector_in, slot_value, face_width):
    return lax.dynamic_slice_in_dim(vector_in, slot_value * face_width, face_width, 0)


def place_faces(vector_in, slot_list, incoming, face_width):
    for facing in range(4):
        first_row = slot_list[facing] * face_width
        current = lax.dynamic_slice_in_dim(vector_in, first_row, face_width, 0)
        vector_in = lax.dynamic_update_slice_in_dim(
            vector_in, current + incoming[facing], first_row, 0
        )
    return vector_in


def assemble(contrib, slot_list, face_width):
    outgoing = [face_rows(contrib, slot_list[facing], face_width) for facing in range(4)]
    incoming = [None, None, None, None]
    for offset, sender, getter in ((1, 1, 0), (-1, 0, 1)):
        incoming[getter] = shifted(outgoing[sender], "region", offset)
    for offset, sender, getter in ((1, 3, 2), (-1, 2, 3)):
        incoming[getter] = shifted(outgoing[sender], "block", offset)
    return place_faces(contrib, slot_list, incoming, face_width)


def gather_coefficients(coeffs):
    return lax.all_gather(coeffs, ("region", "block"), axis=0, tiled=True)


def body(
    gap_terms,
    rigid_loads,
    dual_matrix,
    dirichlet_matrix,
    rigid_modes,
    coarse_rows,
    face_slot,
    glue_sign,
):
    face_width = FACE
    glue_float = glue_sign[0, 0].astype(jnp.float32)[:, None]
    slot_list = face_slot[0, 0]
    signed_modes = rigid_modes[0, 0] * glue_float[:, 0][None, :]
    own_rows = coarse_rows[0, 0]
    dual_block = dual_matrix[0, 0]
    dirichlet_block = dirichlet_matrix[0, 0]
    region_at = lax.axis_index("region")
    block_at = lax.axis_index("block")
    present = [
        region_at > 0,
        region_at < lax.axis_size("region") - 1,
        block_at > 0,
        block_at < lax.axis_size("block") - 1,
    ]
    positions = jnp.arange(signed_modes.shape[1]) // face_width
    share_weight = jnp.ones(positions.shape, jnp.float32)
    for facing in range(4):
        share_weight = jnp.where(
            (positions == slot_list[facing]) & present[facing], 0.5, share_weight
        )
    share_weight = share_weight[:, None]

    def rigid_field(gathered):
        amplitude = jnp.dot(
            own_rows, gathered, precision=precise, preferred_element_type=jnp.float32
        )
        contrib = jnp.einsum("ki,kn->in", signed_modes, amplitude, precision=precise)
        return assemble(contrib, slot_list, face_width)

    def coefficients_of(vector_in):
        return jnp.dot(
            signed_modes, vector_in, precision=precise, preferred_element_type=jnp.float32
        )

    def signed_product(matrix, vector_in):
        lowered = (glue_float * vector_in).astype(jnp.bfloat16)
        return glue_float * jnp.dot(matrix, lowered, preferred_element_type=jnp.float32)

    def partial_inner(left_side, right_side):
        return jnp.sum(share_weight * left_side * right_side, axis=0, keepdims=True)

    def global_inner(left_side, right_side):
        return lax.psum(partial_inner(left_side, right_side), ("region", "block"))

    multiplier = rigid_field(gather_coefficients(rigid_loads[0, 0]))
    residual = assemble(
        gap_terms[0, 0] - signed_product(dual_block, multiplier), slot_list, face_width
    )
    residual_coeffs = gather_coefficients(coefficients_of(residual))
    search = residual - rigid_field(residual_coeffs)
    direction = search
    energy_last = None
    for iteration in range(ITERS):
        final_turn = iteration == ITERS - 1
        precond = assemble(
            share_weight * signed_product(dirichlet_block, share_weight * search),
            slot_list,
            face_width,
        )
        projected = precond - rigid_field(gather_coefficients(coefficients_of(precond)))
        energy_now = global_inner(search, projected)
        if iteration == 0:
            direction = projected
        else:
            direction = projected + energy_now / energy_last * direction
        operated = assemble(signed_product(dual_block, direction), slot_list, face_width)
        curvature = global_inner(direction, operated)
        step_size = energy_now / curvature
        multiplier = multiplier + step_size * direction
        if not final_turn:
            residual = residual - step_size * operated
            residual_coeffs = gather_coefficients(coefficients_of(residual))
            search = residual - rigid_field(residual_coeffs)
        energy_last = energy_now
    return multiplier[None, None]


def solution(mesh):
    in_specs = (
        P("region", "block", None, None),
        P("region", "block", None, None),
        P("region", "block", None, None),
        P("region", "block", None, None),
        P("region", "block", None, None),
        P("region", "block", None, None),
        P("region", "block", None),
        P("region", "block", None),
    )
    out_specs = P("region", "block", None, None)
    return jax.shard_map(body, mesh=mesh, in_specs=in_specs, out_specs=out_specs, check_vma=False)
```

profile of v0, /device:TPU:1, one launch (start us, length us, event | category | flops | bytes accessed | tf_op | source)
XLA Modules:
  0.0 793.9 jit_solution(2967096194098549107)
XLA Ops:
  2.9 79.1 %all-gather = f32[1,1,1536,128]{3,1,0,2:T(1,128)S(1)} all-gather(f32[1,1,6,128]{3,1,0,2:T(1,128)} %bitcast.146), channel_id=2, replica_groups=mesh['region'=16,'block'=16] {'region','block'}, dimensions={2}, use_global_device_ids=true | all-gather | bytes 789504 | tf_op jit(solution)/shard_map/all_gather | solution.py:44
  99.7 4.2 fusion.34
  103.9 4.7 collective-permute-start.4
  114.5 4.6 collective-permute-start.6
  121.6 70.4 %all-gather.1 = f32[256,6,128]{2,1,0:T(8,128)S(1)} all-gather(f32[1,6,128]{2,1,0:T(8,128)S(1)} %convolution_bitcast_fusion.3), channel_id=1, replica_groups=mesh['region'=16,'block'=16] {'region','block'}, dimensions={0}, use_global_device_ids=true | all-gather | bytes 789504 | tf_op jit(solution)/shard_map/all_gather | solution.py:44
  205.2 4.0 collective-permute-start.10
  210.7 3.9 fusion.25
  214.7 4.7 collective-permute-start.12
  221.4 4.6 collective-permute-start.14
  227.4 4.6 collective-permute-done.13
  232.6 71.5 %all-gather.2 = f32[256,6,128]{2,1,0:T(8,128)} all-gather(f32[1,6,128]{2,1,0:T(8,128)S(1)} %convolution_bitcast_fusion.2), channel_id=1, replica_groups=mesh['region'=16,'block'=16] {'region','block'}, dimensions={0}, use_global_device_ids=true | all-gather | bytes 789504 | tf_op jit(solution)/shard_map/all_gather | solution.py:44
  315.7 4.1 collective-permute-start.18
  325.8 4.7 collective-permute-start.20
  332.4 4.6 collective-permute-start.22
  338.5 4.6 collective-permute-done.21
  343.6 82.2 %all-reduce = (f32[1,128]{1,0:T(1,128)S(1)}, f32[1,128]{1,0:T(1,128)S(1)}) all-reduce(f32[1,128]{1,0:T(1,128)S(1)} %bitcast.148, f32[1,128]{1,0:T(1,128)S(1)} %bitcast.147), channel_id=1, replica_groups=mesh['region'=16,'block'=16] {'region','block'}, use_global_device_ids=true, to_apply=%region_1.2 | all-reduce | flops 256 | bytes 2048 | tf_op jit(solution)/shard_map/psum | solution.py:100
  426.3 64.5 %all-gather.3 = f32[256,6,128]{2,1,0:T(8,128)} all-gather(f32[1,6,128]{2,1,0:T(8,128)S(1)} %convolution_bitcast_fusion.1), channel_id=1, replica_groups=mesh['region'=16,'block'=16] {'region','block'}, dimensions={0}, use_global_device_ids=true | all-gather | bytes 789504 | tf_op jit(solution)/shard_map/all_gather | solution.py:44
  512.9 4.7 collective-permute-start.28
  519.6 4.6 collective-permute-start.30
  525.7 4.3 collective-permute-done.29
  530.6 67.1 %all-gather.4 = f32[256,6,128]{2,1,0:T(8,128)S(1)} all-gather(f32[1,6,128]{2,1,0:T(8,128)S(1)} %convolution_bitcast_fusion), channel_id=1, replica_groups=mesh['region'=16,'block'=16] {'region','block'}, dimensions={0}, use_global_device_ids=true | all-gather | bytes 789504 | tf_op jit(solution)/shard_map/all_gather | solution.py:44
  615.7 81.3 %psum.30 = f32[1,128]{1,0:T(1,128)S(1)} all-reduce(f32[1,128]{1,0:T(1,128)S(1)} %bitcast.150), channel_id=1, replica_groups=mesh['region'=16,'block'=16] {'region','block'}, use_global_device_ids=true, to_apply=%region_5.6 | all-reduce | flops 128 | bytes 1024 | tf_op jit(solution)/shard_map/psum | solution.py:100
  709.7 5.8 collective-permute-done.37
  715.9 76.7 %psum.31 = f32[1,128]{1,0:T(1,128)S(1)} all-reduce(f32[1,128]{1,0:T(1,128)S(1)} %bitcast.149), channel_id=1, replica_groups=mesh['region'=16,'block'=16] {'region','block'}, use_global_device_ids=true, to_apply=%region_7.8 | all-reduce | flops 128 | bytes 1024 | tf_op jit(solution)/shard_map/psum | solution.py:100
  (163 shorter events, 124.3 us)
Async XLA Ops:
  92.1 7.5 collective-permute-start.3
  103.9 7.3 collective-permute-start.4
  111.2 7.9 collective-permute-start.5
  112.5 8.5 %collective-permute-start.7 = (f32[256,128]{1,0:T(8,128)S(1)}, f32[256,128]{1,0:T(8,128)S(1)}, u32[]{:S(2)}, u32[]{:S(2)}) collective-permute-start(f32[256,128]{1,0:T(8,128)S(1)} %get-tuple-element.43), channel_id=1, source_target_pairs={{1,0},{2,1},{3,2},{4,3},{5,4},{6,5},{7,6},{8,7},{9,8},{10,9},{11,1... | collective-permute-start | bytes 393224 | tf_op jit(solution)/shard_map/ppermute | solution.py:16
  198.5 10.7 %collective-permute-start.9 = (f32[256,128]{1,0:T(8,128)S(1)}, f32[256,128]{1,0:T(8,128)S(1)}, u32[]{:S(2)}, u32[]{:S(2)}) collective-permute-start(f32[256,128]{1,0:T(8,128)S(1)} %get-tuple-element.42), channel_id=1, source_target_pairs={{16,0},{32,16},{48,32},{64,48},{80,64},{96,80},{112,96},{128,112},... | collective-permute-start | bytes 393224 | tf_op jit(solution)/shard_map/ppermute | solution.py:16
  202.3 8.4 %collective-permute-start.11 = (f32[256,128]{1,0:T(8,128)S(1)}, f32[256,128]{1,0:T(8,128)S(1)}, u32[]{:S(2)}, u32[]{:S(2)}) collective-permute-start(f32[256,128]{1,0:T(8,128)S(1)} %get-tuple-element.39), channel_id=1, source_target_pairs={{1,0},{2,1},{3,2},{4,3},{5,4},{6,5},{7,6},{8,7},{9,8},{10,9},{11,1... | collective-permute-start | bytes 393224 | tf_op jit(solution)/shard_map/ppermute | solution.py:16
  214.7 12.7 %collective-permute-start.12 = (f32[256,128]{1,0:T(8,128)S(1)}, f32[256,128]{1,0:T(8,128)S(1)}, u32[]{:S(2)}, u32[]{:S(2)}) collective-permute-start(f32[256,128]{1,0:T(8,128)S(1)} %get-tuple-element.37), channel_id=1, source_target_pairs={{0,16},{16,32},{32,48},{48,64},{64,80},{80,96},{96,112},{112,128},... | collective-permute-start | bytes 393224 | tf_op jit(solution)/shard_map/ppermute | solution.py:16
  219.4 12.6 %collective-permute-start.15 = (f32[256,128]{1,0:T(8,128)S(1)}, f32[256,128]{1,0:T(8,128)S(1)}, u32[]{:S(2)}, u32[]{:S(2)}) collective-permute-start(f32[256,128]{1,0:T(8,128)S(1)} %get-tuple-element.35), channel_id=1, source_target_pairs={{1,0},{2,1},{3,2},{4,3},{5,4},{6,5},{7,6},{8,7},{9,8},{10,9},{11,1... | collective-permute-start | bytes 393224 | tf_op jit(solution)/shard_map/ppermute | solution.py:16
  221.4 10.7 %collective-permute-start.14 = (f32[256,128]{1,0:T(8,128)S(1)}, f32[256,128]{1,0:T(8,128)S(1)}, u32[]{:S(2)}, u32[]{:S(2)}) collective-permute-start(f32[256,128]{1,0:T(8,128)S(1)} %get-tuple-element.36), channel_id=1, source_target_pairs={{0,1},{1,2},{2,3},{3,4},{4,5},{5,6},{6,7},{7,8},{8,9},{9,10},{10,1... | collective-permute-start | bytes 393224 | tf_op jit(solution)/shard_map/ppermute | solution.py:16
  311.6 8.2 %collective-permute-start.17 = (f32[256,128]{1,0:T(8,128)S(1)}, f32[256,128]{1,0:T(8,128)S(1)}, u32[]{:S(2)}, u32[]{:S(2)}) collective-permute-start(f32[256,128]{1,0:T(8,128)S(1)} %get-tuple-element.34), channel_id=1, source_target_pairs={{16,0},{32,16},{48,32},{64,48},{80,64},{96,80},{112,96},{128,112},... | collective-permute-start | bytes 393224 | tf_op jit(solution)/shard_map/ppermute | solution.py:16
  312.9 8.9 %collective-permute-start.19 = (f32[256,128]{1,0:T(8,128)S(1)}, f32[256,128]{1,0:T(8,128)S(1)}, u32[]{:S(2)}, u32[]{:S(2)}) collective-permute-start(f32[256,128]{1,0:T(8,128)S(1)} %get-tuple-element.31), channel_id=1, source_target_pairs={{1,0},{2,1},{3,2},{4,3},{5,4},{6,5},{7,6},{8,7},{9,8},{10,9},{11,1... | collective-permute-start | bytes 393224 | tf_op jit(solution)/shard_map/ppermute | solution.py:16
  325.8 12.7 %collective-permute-start.20 = (f32[256,128]{1,0:T(8,128)S(1)}, f32[256,128]{1,0:T(8,128)S(1)}, u32[]{:S(2)}, u32[]{:S(2)}) collective-permute-start(f32[256,128]{1,0:T(8,128)S(1)} %get-tuple-element.29), channel_id=1, source_target_pairs={{0,16},{16,32},{32,48},{48,64},{64,80},{80,96},{96,112},{112,128},... | collective-permute-start | bytes 393224 | tf_op jit(solution)/shard_map/ppermute | solution.py:16
  330.5 12.6 %collective-permute-start.23 = (f32[256,128]{1,0:T(8,128)S(1)}, f32[256,128]{1,0:T(8,128)S(1)}, u32[]{:S(2)}, u32[]{:S(2)}) collective-permute-start(f32[256,128]{1,0:T(8,128)S(1)} %get-tuple-element.27), channel_id=1, source_target_pairs={{1,0},{2,1},{3,2},{4,3},{5,4},{6,5},{7,6},{8,7},{9,8},{10,9},{11,1... | collective-permute-start | bytes 393224 | tf_op jit(solution)/shard_map/ppermute | solution.py:16
  332.4 10.7 %collective-permute-start.22 = (f32[256,128]{1,0:T(8,128)S(1)}, f32[256,128]{1,0:T(8,128)S(1)}, u32[]{:S(2)}, u32[]{:S(2)}) collective-permute-start(f32[256,128]{1,0:T(8,128)S(1)} %get-tuple-element.28), channel_id=1, source_target_pairs={{0,1},{1,2},{2,3},{3,4},{4,5},{5,6},{6,7},{7,8},{8,9},{9,10},{10,1... | collective-permute-start | bytes 393224 | tf_op jit(solution)/shard_map/ppermute | solution.py:16
  501.1 7.5 collective-permute-start.27
  512.9 12.7 %collective-permute-start.28 = (f32[256,128]{1,0:T(8,128)S(1)}, f32[256,128]{1,0:T(8,128)S(1)}, u32[]{:S(2)}, u32[]{:S(2)}) collective-permute-start(f32[256,128]{1,0:T(8,128)S(1)} %get-tuple-element.21), channel_id=1, source_target_pairs={{0,16},{16,32},{32,48},{48,64},{64,80},{80,96},{96,112},{112,128},... | collective-permute-start | bytes 393224 | tf_op jit(solution)/shard_map/ppermute | solution.py:16
  517.7 12.4 %collective-permute-start.31 = (f32[256,128]{1,0:T(8,128)S(1)}, f32[256,128]{1,0:T(8,128)S(1)}, u32[]{:S(2)}, u32[]{:S(2)}) collective-permute-start(f32[256,128]{1,0:T(8,128)S(1)} %get-tuple-element.19), channel_id=1, source_target_pairs={{1,0},{2,1},{3,2},{4,3},{5,4},{6,5},{7,6},{8,7},{9,8},{10,9},{11,1... | collective-permute-start | bytes 393224 | tf_op jit(solution)/shard_map/ppermute | solution.py:16
  519.6 10.4 %collective-permute-start.30 = (f32[256,128]{1,0:T(8,128)S(1)}, f32[256,128]{1,0:T(8,128)S(1)}, u32[]{:S(2)}, u32[]{:S(2)}) collective-permute-start(f32[256,128]{1,0:T(8,128)S(1)} %get-tuple-element.20), channel_id=1, source_target_pairs={{0,1},{1,2},{2,3},{3,4},{4,5},{5,6},{6,7},{7,8},{8,9},{9,10},{10,1... | collective-permute-start | bytes 393224 | tf_op jit(solution)/shard_map/ppermute | solution.py:16
  606.1 7.6 collective-permute-start.33
  607.4 8.1 %collective-permute-start.35 = (f32[256,128]{1,0:T(8,128)S(1)}, f32[256,128]{1,0:T(8,128)S(1)}, u32[]{:S(2)}, u32[]{:S(2)}) collective-permute-start(f32[256,128]{1,0:T(8,128)S(1)} %get-tuple-element.15), channel_id=1, source_target_pairs={{1,0},{2,1},{3,2},{4,3},{5,4},{6,5},{7,6},{8,7},{9,8},{10,9},{11,1... | collective-permute-start | bytes 393224 | tf_op jit(solution)/shard_map/ppermute | solution.py:16
  701.0 8.7 %collective-permute-start.36 = (f32[256,128]{1,0:T(8,128)S(1)}, f32[256,128]{1,0:T(8,128)S(1)}, u32[]{:S(2)}, u32[]{:S(2)}) collective-permute-start(f32[256,128]{1,0:T(8,128)S(1)} %get-tuple-element.13), channel_id=1, source_target_pairs={{0,16},{16,32},{32,48},{48,64},{64,80},{80,96},{96,112},{112,128},... | collective-permute-start | bytes 393224 | tf_op jit(solution)/shard_map/ppermute | solution.py:16
  702.4 13.1 %collective-permute-start.39 = (f32[256,128]{1,0:T(8,128)S(1)}, f32[256,128]{1,0:T(8,128)S(1)}, u32[]{:S(2)}, u32[]{:S(2)}) collective-permute-start(f32[256,128]{1,0:T(8,128)S(1)} %get-tuple-element.11), channel_id=1, source_target_pairs={{1,0},{2,1},{3,2},{4,3},{5,4},{6,5},{7,6},{8,7},{9,8},{10,9},{11,1... | collective-permute-start | bytes 393224 | tf_op jit(solution)/shard_map/ppermute | solution.py:16
  705.3 10.2 %collective-permute-start.38 = (f32[256,128]{1,0:T(8,128)S(1)}, f32[256,128]{1,0:T(8,128)S(1)}, u32[]{:S(2)}, u32[]{:S(2)}) collective-permute-start(f32[256,128]{1,0:T(8,128)S(1)} %get-tuple-element.12), channel_id=1, source_target_pairs={{0,1},{1,2},{2,3},{3,4},{4,5},{5,6},{6,7},{7,8},{8,9},{9,10},{10,1... | collective-permute-start | bytes 393224 | tf_op jit(solution)/shard_map/ppermute | solution.py:16
  708.3 7.2 collective-permute-start.37
  (21 other events, 393.4 us)
where the time goes:
time: 804 us; the launch traced here: 794 us
  blocking collectives  593 us (74%)
  starting transfers between devices  106 us (13%)
  waiting for transfers between devices  44.6 us (6%)
  matrix products  33.9 us (4%)
    all_gather x5, blocking collectives, gather_coefficients(): return lax.all_gather(coeffs, ('region', 'block'), axis=0, tiled=True)  353 us
    psum x3, blocking collectives, global_inner(): return lax.psum(partial_inner(left_side, right_side), ('region', 'block'))  240 us
    ppermute x40, starting transfers between devices, shifted(): return lax.ppermute(block, axis, route)  106 us
    ppermute x40, waiting for transfers between devices, shifted(): return lax.ppermute(block, axis, route)  44.6 us
    dot_general x5, matrix products, signed_product(): jnp.dot(matrix, lowered, preferred_element_type=jnp.float32)  19.6 us
  transfers between devices with their start and end apart: 40, of which 18 were waited for; matrix products, arithmetic and copies ran while one was open for 0% of the time, Pallas kernels for 0%

commit v1 on v0

v1 whole, which is shorter than its diff:
```python
import jax
import jax.numpy as jnp
from jax import lax
from jax.experimental import pallas as pl
from jax.experimental.pallas import tpu as pltpu
from jax.sharding import PartitionSpec as P

FACE = 256
SLOTS = 6
NL = FACE * SLOTS
NRHS = 128
NR = 16
NBK = 16
ROUNDS = 5

f32 = jnp.float32
bf16 = jnp.bfloat16
MESH = pl.DeviceIdType.MESH


def split(x):
    hi = x.astype(bf16)
    lo = (x - hi.astype(f32)).astype(bf16)
    return hi, lo


def dot(a, b):
    return jnp.dot(a, b, preferred_element_type=f32)


def kernel(
    slot_ref, gap_hbm, loads_ref, dual_hbm, diri_hbm, modes_ref, coarse_ref, glue_ref,
    out_ref,
    dmat, emat, gap_v, glue_b, m16, mt, coarse8, kown, kown16, kdist, khi, klo,
    lam, search, direc, wloc, field, low, pbuf, xbuf, abuf,
    g1_out, g1_in, g1_all, s1_out, s1_in, s2_out, s2_in, s3_out, s3_in,
    a_out, al_all, face_out, face_in, f_out, f_in,
    load_sem, kd_send, kd_recv, st_send, st_recv, a_send, a_recv, fc_send, fc_recv,
):
    region = lax.axis_index("region")
    block = lax.axis_index("block")
    present = [region > 0, region < NR - 1, block > 0, block < NBK - 1]
    peer = [
        {"region": region - 1}, {"region": region + 1},
        {"block": block - 1}, {"block": block + 1},
    ]

    def rows8(index):
        return pl.ds(pl.multiple_of(index * 8, 8), 8)

    loads = [
        pltpu.make_async_copy(gap_hbm, gap_v, load_sem.at[0]),
        pltpu.make_async_copy(dual_hbm, dmat, load_sem.at[1]),
        pltpu.make_async_copy(diri_hbm, emat, load_sem.at[2]),
    ]
    for copy in loads:
        copy.start()

    for ref in al_all:
        ref[...] = jnp.zeros_like(ref)
    for ref in face_in:
        ref[4] = jnp.zeros((FACE, NRHS), f32)
    for f in range(4):
        @pl.when(jnp.logical_not(present[f]))
        def _():
            for ref in face_in:
                ref[f] = jnp.zeros((FACE, NRHS), f32)

    barrier = pltpu.get_barrier_semaphore()

    def greet(p, carry):
        pl.semaphore_signal(
            barrier, inc=1, device_id={"block": lax.rem(block + p, NBK)}, device_id_type=MESH
        )
        pl.semaphore_signal(
            barrier, inc=1, device_id={"region": lax.rem(region + p, NR)}, device_id_type=MESH
        )
        return carry

    lax.fori_loop(1, 16, greet, 0)

    g1_out[...] = jnp.zeros_like(g1_out)
    g1_out[0:6, :] = loads_ref[...]
    coarse8[...] = jnp.zeros_like(coarse8)
    coarse8[0:6, :] = coarse_ref[...]
    row_i = lax.broadcasted_iota(jnp.int32, (96, 128), 0)
    lane_i = lax.broadcasted_iota(jnp.int32, (96, 128), 1)
    spread = ((row_i == (lane_i >> 3) * 6 + (lane_i & 7)) & ((lane_i & 7) < 6)).astype(f32)
    row_8 = lax.broadcasted_iota(jnp.int32, (8, 128), 0)
    lane_8 = lax.broadcasted_iota(jnp.int32, (8, 128), 1)
    lane_blk = lane_8 >> 3
    passing = ((row_8 >= 6) & ((lane_8 & 7) == row_8)).astype(f32)
    for r in range(NR):
        piece = coarse8[:, 96 * r:96 * r + 96]
        wide = jnp.dot(piece, spread, preferred_element_type=f32, precision=lax.Precision.HIGHEST)
        kown[r] = wide + passing
    pl.semaphore_wait(barrier, 30)

    def all_to(axis, me, count, src, dst, send_sem, recv_sem):
        def one(p, carry):
            to = lax.rem(me + p, count)
            pltpu.make_async_remote_copy(
                src_ref=src(to), dst_ref=dst.at[me], send_sem=send_sem, recv_sem=recv_sem,
                device_id={axis: to}, device_id_type=MESH,
            ).start()
            return carry

        lax.fori_loop(1, count, one, 0)

    def await_all(dst, sem):
        part = dst.at[pl.ds(0, 15)]
        pltpu.make_async_copy(part, part, sem).wait()

    all_to("block", block, NBK, lambda to: g1_out, g1_in, st_send.at[0, 0], st_recv.at[0, 0])
    all_to("block", block, NBK, lambda to: kown, kdist, kd_send, kd_recv)
    g1_in[block] = g1_out[...]
    kdist[block] = kown[...]
    for r in range(NR):
        piece = kown[r]
        hi = piece.astype(bf16).astype(f32)
        kown16[:, 128 * r:128 * r + 128] = jnp.concatenate([hi, piece - hi], axis=0).astype(bf16)

    for i in range(NL // 128):
        signs = glue_ref[0:1, 128 * i:128 * i + 128].astype(f32)
        glue_b[128 * i:128 * i + 128, :] = jnp.broadcast_to(signs, (128, 128)).T
        signed = jnp.concatenate(
            [modes_ref[:, 128 * i:128 * i + 128] * signs, jnp.zeros((2, 128), f32)], axis=0
        )
        hi = signed.astype(bf16).astype(f32)
        m16[:, 128 * i:128 * i + 128] = jnp.concatenate([hi, signed - hi], axis=0).astype(bf16)
        stacked = jnp.concatenate(
            [hi, hi, signed - hi, jnp.zeros((104, 128), f32)], axis=0
        ).T
        mt[128 * i:128 * i + 128, :] = stacked[:, 0:32].astype(bf16)

    facing = []
    share = []
    for j in range(SLOTS):
        where = jnp.int32(4)
        weight = jnp.float32(1.0)
        for f in range(4):
            hit = slot_ref[0, f] == j
            where = jnp.where(hit, f, where)
            weight = jnp.where(jnp.logical_and(hit, present[f]), 0.5, weight)
        facing.append(where)
        share.append(weight)

    def swap_amplitudes(k, others):
        for f in others:
            @pl.when(present[f])
            def _(f=f):
                pltpu.make_async_remote_copy(
                    src_ref=a_out.at[k], dst_ref=al_all[k].at[f ^ 1],
                    send_sem=a_send.at[k, f], recv_sem=a_recv.at[k, f ^ 1],
                    device_id=peer[f], device_id_type=MESH,
                ).start()

    def amplitude_done(k, others):
        for f in others:
            @pl.when(present[f])
            def _(f=f):
                pltpu.make_async_copy(a_out.at[k], al_all[k].at[f], a_recv.at[k, f]).wait()

    def field_slot(k, j):
        q = a_out[k] - al_all[k][facing[j]]
        hi = q.astype(bf16).astype(f32)
        stacked = jnp.concatenate([hi, q - hi, hi, jnp.zeros_like(q)], axis=0).astype(bf16)
        return dot(mt[FACE * j:FACE * j + FACE, :], stacked)

    def product(matrix, j):
        rows = slice(FACE * j, FACE * j + FACE)
        return glue_b[rows, :] * dot(matrix[rows, :], low[...])

    def lower(j, value):
        rows = slice(FACE * j, FACE * j + FACE)
        low[rows, :] = (glue_b[rows, :] * value).astype(bf16)

    await_all(g1_in, st_recv.at[0, 0])
    all_to("region", region, NR, lambda to: g1_in, g1_all, st_send.at[0, 1], st_recv.at[0, 1])
    g1_all[region] = g1_in[...]
    await_all(g1_all, st_recv.at[0, 1])
    total = jnp.zeros((16, NRHS), f32)
    for r in range(0, NR, 2):
        pair = g1_all[r:r + 2].reshape(256, NRHS)
        hi, lo = split(pair)
        rows = kown16[:, 128 * r:128 * r + 256]
        total = total + (dot(rows, hi) + dot(rows, lo))
    a_out[0] = total[:8] + total[8:]
    swap_amplitudes(0, range(4))
    loads[0].wait()
    loads[1].wait()
    amplitude_done(0, range(4))
    for j in range(SLOTS):
        value = field_slot(0, j)
        lam[j] = value
        lower(j, value)
    for j in range(SLOTS):
        wloc[j] = gap_v[FACE * j:FACE * j + FACE, :] - product(dmat, j)

    xbuf[...] = jnp.zeros_like(xbuf)

    def coarse_round(k, extra, prepare=None):
        mine = extra
        for j in range(SLOTS):
            hi, lo = split(wloc[j])
            rows = m16[:, FACE * j:FACE * j + FACE]
            part = dot(rows, hi) + dot(rows, lo)
            part = part[:8] + part[8:]
            pbuf[j] = part
            mine = part if mine is None else mine + part
        xbuf[rows8(block), :] = mine
        place = [lax.rem(block + 8, 16), lax.rem(block + 9, 16), block - 1, block + 1]
        for f in range(4):
            part = pbuf[slot_ref[0, f]]

            @pl.when(present[f])
            def _(f=f, part=part):
                xbuf[rows8(place[f]), :] = -part
        s1_out[k] = xbuf[...].T.reshape(16, 8, 128)
        all_to(
            "block", block, NBK, lambda to: s1_out.at[k, to], s1_in.at[k],
            st_send.at[k, 0], st_recv.at[k, 0],
        )
        s1_in[k, block] = s1_out[k, block]
        for f in range(4):
            face_out[k - 1, f] = wloc[slot_ref[0, f]]
        await_all(s1_in.at[k], st_recv.at[k, 0])
        main = jnp.zeros((8, 128), f32)
        before = jnp.zeros((8, 128), f32)
        after = jnp.zeros((8, 128), f32)
        for t in range(NBK):
            tile = s1_in[k, t]
            main = main + jnp.where((lane_blk >= t - 1) & (lane_blk <= t + 1), tile, 0.0)
            before = before + jnp.where(lane_blk == (t + 8) % 16, tile, 0.0)
            after = after + jnp.where(lane_blk == (t + 9) % 16, tile, 0.0)
        s2_out[k, 0] = main
        s2_out[k, 1] = pltpu.roll(before, 64, 1)
        s2_out[k, 2] = pltpu.roll(after, 56, 1)
        all_to(
            "region", region, NR, lambda to: s2_out.at[k], s2_in.at[k],
            st_send.at[k, 1], st_recv.at[k, 1],
        )
        s2_in[k, region] = s2_out[k]
        for f in range(4):
            @pl.when(present[f])
            def _(f=f):
                pltpu.make_async_remote_copy(
                    src_ref=face_out.at[k - 1, f], dst_ref=face_in[k - 1].at[f ^ 1],
                    send_sem=fc_send.at[k - 1, f], recv_sem=fc_recv.at[k - 1, f ^ 1],
                    device_id=peer[f], device_id_type=MESH,
                ).start()
        if prepare is not None:
            prepare()
        await_all(s2_in.at[k], st_recv.at[k, 1])
        pieces = []
        for r in range(NR):
            tile = s2_in[k, r, 0]
            if r < NR - 1:
                tile = tile + s2_in[k, r + 1, 1]
            if r > 0:
                tile = tile + s2_in[k, r - 1, 2]
            hi = tile.astype(bf16).astype(f32)
            pieces.append(jnp.concatenate([hi, tile - hi], axis=0).astype(bf16))
        left = jnp.concatenate(pieces, axis=1)
        both = dot(left, khi[...]) + dot(left, klo[...])
        s3_out[k] = both[:8] + both[8:]
        all_to(
            "block", block, NBK, lambda to: s3_out.at[k], s3_in.at[k],
            st_send.at[k, 2], st_recv.at[k, 2],
        )
        s3_in[k, block] = s3_out[k]
        await_all(s3_in.at[k], st_recv.at[k, 2])
        abuf[...] = s3_in[k].reshape(128, 128).T
        a_out[k] = abuf[rows8(block), :]
        swap_amplitudes(k, range(2))
        for f, near in ((2, block - 1), (3, block + 1)):
            @pl.when(present[f])
            def _(f=f, near=near):
                al_all[k][f] = abuf[rows8(near), :]
        for f in range(4):
            @pl.when(present[f])
            def _(f=f):
                pltpu.make_async_copy(
                    face_out.at[k - 1, f], face_in[k - 1].at[f], fc_recv.at[k - 1, f]
                ).wait()
        amplitude_done(k, range(2))

    def assembled(k, j):
        return wloc[j] + face_in[k - 1][facing[j]] - field_slot(k, j)

    def inner(total, left, right):
        return total + jnp.sum((left * right).reshape(FACE // 8, 8, NRHS), axis=0)

    def finish(total):
        return jnp.sum(total, axis=0, keepdims=True)

    zero8 = jnp.zeros((8, NRHS), f32)

    def coarse_matrix():
        part = kdist.at[pl.ds(0, 15)]
        pltpu.make_async_copy(part, part, kd_recv).wait()
        for r in range(NR):
            hi, lo = split(kdist[:, r].reshape(128, 128).T)
            khi[128 * r:128 * r + 128, :] = hi
            klo[128 * r:128 * r + 128, :] = lo

    coarse_round(1, None, coarse_matrix)
    for j in range(SLOTS):
        value = assembled(1, j)
        search[j] = value
        lower(j, share[j] * value)
    loads[2].wait()
    for j in range(SLOTS):
        wloc[j] = share[j] * product(emat, j)

    coarse_round(2, None)
    energy = zero8
    for j in range(SLOTS):
        value = assembled(2, j)
        direc[j] = value
        lower(j, value)
        energy = inner(energy, share[j] * search[j], value)
    curvature = zero8
    for j in range(SLOTS):
        value = product(dmat, j)
        wloc[j] = value
        field[j] = value
        curvature = inner(curvature, direc[j], value)

    sums = jnp.concatenate([jnp.zeros((6, NRHS), f32), finish(energy), finish(curvature)], axis=0)
    coarse_round(3, sums)
    energy0 = a_out[3, 6:7, :]
    curvature0 = a_out[3, 7:8, :]
    step0 = energy0 / curvature0
    for j in range(SLOTS):
        value = search[j] - step0 * assembled(3, j)
        search[j] = value
        lower(j, share[j] * value)
    for j in range(SLOTS):
        wloc[j] = share[j] * product(emat, j)

    coarse_round(4, None)
    energy = zero8
    cross = zero8
    for j in range(SLOTS):
        value = assembled(4, j)
        lower(j, value)
        energy = inner(energy, share[j] * search[j], value)
        cross = inner(cross, value, field[j])
        search[j] = value
    curvature = zero8
    for j in range(SLOTS):
        curvature = inner(curvature, search[j], product(dmat, j))
    f_out[0] = jnp.concatenate(
        [finish(energy), finish(curvature), finish(cross), jnp.zeros((5, NRHS), f32)], axis=0
    )
    for stage, (axis, me) in enumerate((("block", block), ("region", region))):
        all_to(
            axis, me, 16, lambda to: f_out.at[stage], f_in.at[stage],
            st_send.at[5, stage], st_recv.at[5, stage],
        )
        f_in[stage, me] = f_out[stage]
        await_all(f_in.at[stage], st_recv.at[5, stage])
        f_out[stage + 1] = jnp.sum(f_in[stage], axis=0)
    energy1 = f_out[2, 0:1, :]
    beta = energy1 / energy0
    curvature1 = f_out[2, 1:2, :] + 2.0 * beta * f_out[2, 2:3, :] + beta * beta * curvature0
    step1 = energy1 / curvature1
    first = step0 + step1 * beta
    for j in range(SLOTS):
        out_ref[FACE * j:FACE * j + FACE, :] = lam[j] + first * direc[j] + step1 * search[j]

    def sent(ref, sem):
        pltpu.make_async_copy(ref, ref, sem).wait()

    sent(g1_in.at[pl.ds(0, 15)], st_send.at[0, 0])
    sent(g1_all.at[pl.ds(0, 15)], st_send.at[0, 1])
    sent(kdist.at[pl.ds(0, 15)], kd_send)
    for k in range(1, ROUNDS):
        sent(s1_in.at[k, pl.ds(0, 15)], st_send.at[k, 0])
        sent(s2_in.at[k, pl.ds(0, 15)], st_send.at[k, 1])
        sent(s3_in.at[k, pl.ds(0, 15)], st_send.at[k, 2])
    for stage in range(2):
        sent(f_in.at[stage, pl.ds(0, 15)], st_send.at[5, stage])
    for f in range(4):
        @pl.when(present[f])
        def _(f=f):
            for k in range(4):
                sent(face_out.at[k, f], fc_send.at[k, f])
            for k in range(ROUNDS):
                if k == 0 or f < 2:
                    sent(a_out.at[k], a_send.at[k, f])


def body(
    gap_terms, rigid_loads, dual_matrix, dirichlet_matrix, rigid_modes, coarse_rows,
    face_slot, glue_sign,
):
    vmem = pl.BlockSpec(memory_space=pltpu.VMEM)
    hbm = pl.BlockSpec(memory_space=pl.ANY)
    V = pltpu.VMEM
    slots = (SLOTS, FACE, NRHS)
    scratch = [
        V((NL, NL), bf16), V((NL, NL), bf16), V((NL, NRHS), f32), V((NL, NRHS), f32),
        V((16, NL), bf16), V((NL, 32), bf16), V((8, NL), f32),
        V((NR, 8, 128), f32), V((16, NR * 128), bf16), V((NBK, NR, 8, 128), f32),
        V((NR * 128, 128), bf16), V((NR * 128, 128), bf16),
        V(slots, f32), V(slots, f32), V(slots, f32), V(slots, f32), V(slots, f32),
        V((NL, NRHS), bf16), V((SLOTS, 8, NRHS), f32), V((128, 128), f32), V((128, 128), f32),
        V((8, 128), f32), V((NBK, 8, 128), f32), V((NR, NBK, 8, 128), f32),
        V((ROUNDS, NBK, 8, 128), f32), V((ROUNDS, NBK, 8, 128), f32),
        V((ROUNDS, 3, 8, 128), f32), V((ROUNDS, NR, 3, 8, 128), f32),
        V((ROUNDS, 8, 128), f32), V((ROUNDS, NBK, 8, 128), f32),
        V((ROUNDS, 8, 128), f32), tuple(V((5, 8, 128), f32) for _ in range(ROUNDS)),
        V((4, 4, FACE, NRHS), f32), tuple(V((5, FACE, NRHS), f32) for _ in range(4)),
        V((3, 8, 128), f32), V((2, 16, 8, 128), f32),
        pltpu.SemaphoreType.DMA((3,)), pltpu.SemaphoreType.DMA, pltpu.SemaphoreType.DMA,
        pltpu.SemaphoreType.DMA((ROUNDS + 1, 3)), pltpu.SemaphoreType.DMA((ROUNDS + 1, 3)),
        pltpu.SemaphoreType.DMA((ROUNDS, 4)), pltpu.SemaphoreType.DMA((ROUNDS, 4)),
        pltpu.SemaphoreType.DMA((4, 4)), pltpu.SemaphoreType.DMA((4, 4)),
    ]
    result = pl.pallas_call(
        kernel,
        out_shape=jax.ShapeDtypeStruct((NL, NRHS), f32),
        in_specs=[
            pl.BlockSpec(memory_space=pltpu.SMEM), hbm, vmem, hbm, hbm, vmem, vmem, vmem,
        ],
        out_specs=vmem,
        scratch_shapes=scratch,
        compiler_params=pltpu.CompilerParams(
            collective_id=0, has_side_effects=True, vmem_limit_bytes=48 * 1024 * 1024,
        ),
        cost_estimate=pl.CostEstimate(
            flops=5 * 2 * NL * NL * NRHS, bytes_accessed=12 * 1024 * 1024, transcendentals=0
        ),
    )(
        face_slot[0], gap_terms[0, 0], rigid_loads[0, 0], dual_matrix[0, 0],
        dirichlet_matrix[0, 0], rigid_modes[0, 0], coarse_rows[0, 0], glue_sign[0],
    )
    return result[None, None]


def solution(mesh):
    matrix = P("region", "block", None, None)
    vector = P("region", "block", None)
    return jax.shard_map(
        body, mesh=mesh, in_specs=(matrix,) * 6 + (vector,) * 2, out_specs=matrix,
        check_vma=False,
    )
```

time: 804 us -> 147 us (0.18); the launches traced: 794 us -> 147 us
  blocking collectives: 593 us -> 0 us
  Pallas kernels: 0 us -> 142 us
  starting transfers between devices: 106 us -> 0 us
  waiting for transfers between devices: 44.6 us -> 0 us
  matrix products: 33.9 us -> 0 us
    all_gather x5 -> x0, blocking collectives: 353 us -> none  [gather_coefficients(): return lax.all_gather(coeffs, ('region', 'block'), axis=0, tiled=True)]
    psum x3 -> x0, blocking collectives: 240 us -> none  [global_inner(): return lax.psum(partial_inner(left_side, right_side), ('region', 'block'))]
    pallas_call x0 -> x1, Pallas kernels: none -> 142 us  [body(): pl.pallas_call(kernel, out_shape=jax.ShapeDtypeStruct((NL, NRHS), f32), i...]
    ppermute x40 -> x0, starting transfers between devices: 106 us -> none  [shifted(): return lax.ppermute(block, axis, route)]
    ppermute x40 -> x0, waiting for transfers between devices: 44.6 us -> none  [shifted(): return lax.ppermute(block, axis, route)]
    dot_general x19 -> x0, matrix products: 33.9 us -> none  [the longest x5 19.6 us: signed_product(): jnp.dot(matrix, lowered, preferred_element_type=jnp.float32)]
  transfers between devices with their start and end apart: 40 -> 0, of which waited for: 18 -> 0; matrix products, arithmetic and copies ran while one was open for 0% -> 0% of each run, Pallas kernels for 0% -> 0%
where the time goes in v1:
time: 147 us
  Pallas kernels  142 us (97%)
  local copies, waits for them, and re-layouts  4.84 us (3%)
    pallas_call x1, Pallas kernels, body(): pl.pallas_call(kernel, out_shape=jax.ShapeDtypeStruct((NL, NRHS), f32), i...  142 us
    unnamed x9, local copies, waits for them, and re-layouts  4.84 us

profile of v1, /device:TPU:1, one launch (start us, length us, event | category | flops | bytes accessed | tf_op | source)
XLA Modules:
  0.0 146.7 jit_solution(1863214726177108588)
XLA Ops:
  0.0 0.7 copy.15
  0.7 0.8 copy_bitcast_fusion
  1.5 0.0 copy-start
  1.5 1.1 copy-done
  2.6 0.0 copy-start.1
  2.6 0.7 copy-done.1
  3.3 0.0 copy-start.2
  3.3 0.7 copy-done.2
  4.0 141.9 %shard_map.82 = f32[1536,128]{1,0:T(8,128)S(1)} custom-call(s32[1,4]{1,0:T(1,128)S(1)} %bitcast.17, f32[1536,128]{1,0:T(8,128)S(1)} %bitcast.15, f32[6,128]{1,0:T(8,128)S(1)} %bitcast.14, bf16[1536,1536]{1,0:T(8,128)(2,1)} %bitcast.18, bf16[1536,1536]{1,0:T(8,128)(2,1)} %bitcast.19, f32[6,1536]{1,0:T(8,128)S(1)} %get-tuple-element.6.modes_ref, ...), custom_call_target="tpu_custom_call" | custom-call | flops 3019898880 | bytes 12582912 | tf_op jit(solution)/shard_map/pallas_call | solution.py:422
  145.8 0.9 copy.17
Async XLA Ops:
  1.5 1.1 copy-start
  2.6 0.7 copy-start.1
  3.3 0.7 copy-start.2

commit v2 on v1

v2 whole, which is shorter than its diff:
```python
import jax
import jax.numpy as jnp
from jax import lax
from jax.experimental import pallas as pl
from jax.experimental.pallas import tpu as pltpu
from jax.sharding import PartitionSpec as P

FACE = 256
SLOTS = 6
NL = FACE * SLOTS
NRHS = 128
NR = 16
NBK = 16
FAR_FIRST = (8, 7, 9, 6, 10, 5, 11, 4, 12, 3, 13, 2, 14, 1, 15)
ROUNDS = 5

f32 = jnp.float32
bf16 = jnp.bfloat16
MESH = pl.DeviceIdType.MESH


def split(x):
    hi = x.astype(bf16)
    lo = (x - hi.astype(f32)).astype(bf16)
    return hi, lo


def dot(a, b):
    return jnp.dot(a, b, preferred_element_type=f32)


def kernel(
    gap_hbm, loads_hbm, dual_hbm, diri_hbm, modes_hbm, coarse_hbm, slot_arg, glue_hbm,
    out_ref,
    loads_ref, modes_ref, coarse_ref, glue_ref,
    dmat, emat, gap_v, glue_b, m16, u16, mt, coarse8, coarse_sib, kpair, kown, kdist, khi, klo,
    dcoef, ecoef, gcoef, ybuf, lown, ldist, lmat, lhi, llo, t_in,
    lam, search, direc, wloc, field, low, pbuf, xbuf, abuf,
    g1_in, g1_all, half_out, half_in, s1_out, s1_in, s2_out, s2_in, s3_out, s3_in,
    a_out, al_all, al_near, part, corr, face_out, face_in, f_out, f_in, c_out, c_in,
    load_sem, kd_send, kd_recv, ld_send, ld_recv, t_send, t_recv, sib_send, sib_recv, st_send, st_recv, a_send, a_recv, fc_send, fc_recv,
):
    region = lax.axis_index("region")
    block = lax.axis_index("block")
    present = [region > 0, region < NR - 1, block > 0, block < NBK - 1]
    peer = [
        {"region": region - 1}, {"region": region + 1},
        {"block": block - 1}, {"block": block + 1},
    ]

    def rows8(index):
        return pl.ds(pl.multiple_of(index * 8, 8), 8)

    slot_ref = slot_arg.at[0]
    core = lax.rem(block, 2)
    place = [lax.rem(block + 8, 16), lax.rem(block + 9, 16), block - 1, block + 1]
    sibling = {"block": block + 1 - 2 * core}
    barrier = pltpu.get_barrier_semaphore()
    for p in range(1, 16):
        pl.semaphore_signal(
            barrier, inc=1, device_id={"block": lax.rem(block + p, NBK)}, device_id_type=MESH
        )
        pl.semaphore_signal(
            barrier, inc=1, device_id={"region": lax.rem(region + p, NR)}, device_id_type=MESH
        )

    loads = [
        pltpu.make_async_copy(source, target, load_sem.at[i])
        for i, (source, target) in enumerate((
            (loads_hbm.at[0], loads_ref), (coarse_hbm.at[0], coarse_ref),
            (glue_hbm.at[0], glue_ref), (modes_hbm.at[0], modes_ref),
            (gap_hbm.at[0, 0], gap_v), (dual_hbm.at[0, 0], dmat), (diri_hbm.at[0, 0], emat),
        ))
    ]
    for copy in loads:
        copy.start()

    pending = []

    def send(src, dst, send_sem, recv_sem, target):
        pltpu.make_async_remote_copy(
            src_ref=src, dst_ref=dst, send_sem=send_sem, recv_sem=recv_sem,
            device_id=target, device_id_type=MESH,
        ).start()

    def all_to(axis, me, src, dst, send_sem, recv_sem):
        for p in FAR_FIRST:
            to = lax.rem(me + p, 16)
            send(src(to), dst.at[me], send_sem, recv_sem, {axis: to})
        pending.append((None, dst.at[pl.ds(0, 15)], send_sem))

    def finished(ref, sem):
        pltpu.make_async_copy(ref, ref, sem).wait()

    def await_all(dst, sem):
        finished(dst.at[pl.ds(0, 15)], sem)

    coarse8[...] = jnp.zeros_like(coarse8)
    loads[1].wait()
    coarse8[0, 0:6, :] = coarse_ref[:, 0, :]
    row_i = lax.broadcasted_iota(jnp.int32, (96, 128), 0)
    lane_i = lax.broadcasted_iota(jnp.int32, (96, 128), 1)
    spread = ((row_i == (lane_i >> 3) * 6 + (lane_i & 7)) & ((lane_i & 7) < 6)).astype(f32)
    row_8 = lax.broadcasted_iota(jnp.int32, (8, 128), 0)
    lane_8 = lax.broadcasted_iota(jnp.int32, (8, 128), 1)
    lane_blk = lane_8 >> 3
    passing = ((row_8 >= 6) & ((lane_8 & 7) == row_8)).astype(f32)
    for r in range(NR):
        piece = coarse8[0, :, 96 * r:96 * r + 96]
        wide = jnp.dot(piece, spread, preferred_element_type=f32, precision=lax.Precision.HIGHEST)
        wide = wide + passing
        kown[r] = wide

    for ref in al_all:
        ref[4] = jnp.zeros((8, NRHS), f32)
    for ref in al_near:
        ref[2] = jnp.zeros((8, NRHS), f32)
    corr[2] = jnp.zeros((FACE, NRHS), f32)
    for ref in face_in:
        ref[4] = jnp.zeros((FACE, NRHS), f32)
    for f in range(4):
        @pl.when(jnp.logical_not(present[f]))
        def _(f=f):
            if f < 2:
                t_in[f] = jnp.zeros((8, 128), f32)
            for ref in al_all:
                ref[f] = jnp.zeros((8, NRHS), f32)
            if f >= 2:
                for ref in al_near:
                    ref[f - 2] = jnp.zeros((8, NRHS), f32)
            for ref in face_in:
                ref[f] = jnp.zeros((FACE, NRHS), f32)

    loads[2].wait()
    loads[3].wait()
    for i in range(NL // 128):
        signs = glue_ref[0:1, 128 * i:128 * i + 128].astype(f32)
        glue_b[128 * i:128 * i + 128, :] = jnp.broadcast_to(signs, (128, 128)).T
        plain = jnp.concatenate(
            [modes_ref[:, 0, 128 * i:128 * i + 128], jnp.zeros((2, 128), f32)], axis=0
        )
        hi = plain.astype(bf16).astype(f32)
        u16[:, 128 * i:128 * i + 128] = jnp.concatenate([hi, plain - hi], axis=0).astype(bf16)
        signed = plain * signs
        hi = signed.astype(bf16).astype(f32)
        m16[:, 128 * i:128 * i + 128] = jnp.concatenate([hi, signed - hi], axis=0).astype(bf16)
        stacked = jnp.concatenate(
            [hi, hi, signed - hi, jnp.zeros((104, 128), f32)], axis=0
        ).T
        half = 128 * (i % 2)
        mt[i // 2, half:half + 128, :] = stacked[:, 0:32].astype(bf16)

    facing = []
    across = []
    beside = []
    share = []
    for j in range(SLOTS):
        where = jnp.int32(4)
        weight = jnp.float32(1.0)
        for f in range(4):
            hit = slot_ref[0, f] == j
            where = jnp.where(hit, f, where)
            weight = jnp.where(jnp.logical_and(hit, present[f]), 0.5, weight)
        facing.append(where)
        across.append(jnp.where(where < 2, where, 2))
        beside.append(jnp.where(jnp.logical_and(where >= 2, where < 4), where - 2, 2))
        share.append(weight)

    def swap_amplitudes(k, others):
        for f in others:
            @pl.when(present[f])
            def _(f=f):
                send(
                    a_out.at[k], al_all[k].at[f ^ 1], a_send.at[k, f], a_recv.at[k, f ^ 1], peer[f]
                )

            pending.append((present[f], a_out.at[k], a_send.at[k, f]))

    def amplitude_done(k, others):
        for f in others:
            @pl.when(present[f])
            def _(f=f):
                pltpu.make_async_copy(a_out.at[k], al_all[k].at[f], a_recv.at[k, f]).wait()

    def spread_modes(modes, q):
        hi = q.astype(bf16).astype(f32)
        stacked = jnp.concatenate([hi, q - hi, hi, jnp.zeros_like(q)], axis=0).astype(bf16)
        return dot(modes, stacked)

    def product(matrix, j):
        rows = slice(FACE * j, FACE * j + FACE)
        return glue_b[rows, :] * dot(matrix[rows, :], low[...])

    def lower(j, value):
        rows = slice(FACE * j, FACE * j + FACE)
        low[rows, :] = (glue_b[rows, :] * value).astype(bf16)

    def add_up(part):
        return part[:8] + part[8:]

    def sums_of(matrix, target, weights):
        for j in range(SLOTS):
            rows = slice(FACE * j, FACE * j + FACE)
            wide = add_up(dot(u16[:, rows], matrix[rows, :])) * weights[j]
            hi = wide.astype(bf16).astype(f32)
            target[16 * j:16 * j + 16, :] = jnp.concatenate([hi, wide - hi], axis=0).astype(bf16)

    def hand_out(mine, all_of, send_sem, recv_sem):
        for p in (8, 6, 10, 4, 12, 2, 14):
            to = {"block": lax.rem(block + p, NBK)}
            send(mine, all_of.at[block], send_sem.at[0], recv_sem.at[0], to)
        send(mine, all_of.at[block], send_sem.at[0], recv_sem.at[0], sibling)
        pending.append((None, all_of.at[pl.ds(0, 8)], send_sem.at[0]))

    def hand_on(all_of, send_sem, recv_sem):
        finished(all_of.at[pl.ds(0, 8)], recv_sem.at[0])
        for p in range(2, 16, 2):
            at = lax.rem(block + p, NBK)
            send(all_of.at[at], all_of.at[at], send_sem.at[1], recv_sem.at[1], sibling)
        pending.append((None, all_of.at[pl.ds(0, 7)], send_sem.at[1]))

    def coupling():
        plain = u16[0:8, :].astype(f32) + u16[8:16, :].astype(f32)
        slot_at = lax.broadcasted_iota(jnp.int32, (8, NL), 1) >> 8
        groups = [plain]
        for f in range(4):
            weight = jnp.where(present[f], -1.0, 0.0)
            groups.append(jnp.where(slot_at == slot_ref[0, f], plain, 0.0) * weight)
        stack = jnp.concatenate(groups + [jnp.zeros((8, NL), f32)], axis=0)
        hi = stack.astype(bf16).astype(f32)
        lo = stack - hi
        wide = dot(jnp.concatenate([hi, lo], axis=0).astype(bf16), dmat[...])
        w_hi, w_lo = split(wide[:48] + wide[48:])
        fill = jnp.zeros((80, NL), f32)
        v_hi = jnp.concatenate([hi, fill], axis=0).astype(bf16)
        v_lo = jnp.concatenate([lo, fill], axis=0).astype(bf16)

        def across_rows(a, b):
            return lax.dot_general(a, b, (((1,), (1,)), ((), ())), preferred_element_type=f32)

        square = across_rows(w_hi, v_hi) + across_rows(w_lo, v_hi) + across_rows(w_hi, v_lo)
        ybuf[...] = jnp.zeros_like(ybuf)
        ybuf[rows8(block), :] = square[0:8]
        for f in range(4):
            @pl.when(present[f])
            def _(f=f):
                ybuf[rows8(place[f]), :] = square[8 * f + 8:8 * f + 16]
        turned = ybuf[...].T
        for g in range(5):
            lown[g] = turned[8 * g:8 * g + 8, :]

    def coupling_send():
        hand_out(lown, ldist, ld_send, ld_recv)
        ldist[block] = lown[...]

    loads[4].wait()
    for j in range(SLOTS):
        rows = slice(FACE * j, FACE * j + FACE)
        hi, lo = split(gap_v[rows, :])
        gcoef[j] = add_up(dot(m16[:, rows], hi) + dot(m16[:, rows], lo))

    own_rows = pl.ds(block * 6, 6)
    loads[0].wait()
    pl.semaphore_wait(barrier, 30)
    for p in FAR_FIRST:
        send(
            loads_ref, g1_in.at[own_rows], st_send.at[0, 0], st_recv.at[0, 0],
            {"block": lax.rem(block + p, NBK)},
        )
    pending.append((None, g1_in.at[pl.ds(0, 90)], st_send.at[0, 0]))
    send(coarse_ref, coarse_sib, sib_send.at[0], sib_recv.at[0], sibling)
    pending.append((None, coarse_sib, sib_send.at[0]))
    g1_in[own_rows] = loads_ref[...]

    loads[5].wait()
    sums_of(dmat, dcoef, [1.0] * SLOTS)
    finished(coarse_sib, sib_recv.at[0])
    coarse8[1, 0:6, :] = coarse_sib[:, 0, :]
    for r in range(NR):
        pieces = []
        for c in range(2):
            piece = coarse8[c, :, 96 * r:96 * r + 96]
            hi = piece.astype(bf16).astype(f32)
            pieces += [hi, piece - hi]
        kpair[r] = jnp.concatenate(pieces, axis=0).astype(bf16)

    finished(g1_in.at[pl.ds(0, 90)], st_recv.at[0, 0])
    for i in (4, 3, 5, 2, 6, 1, 7):
        to = lax.rem(region + 2 * i + core, NR)
        send(
            g1_in, g1_all.at[region], st_send.at[0, 1], st_recv.at[0, 1], {"region": to}
        )

    @pl.when(core == 1)
    def _():
        send(
            g1_in, g1_all.at[region], st_send.at[0, 1], st_recv.at[0, 1],
            {"region": lax.rem(region + 1, NR)},
        )

    pending.append((core == 0, g1_all.at[pl.ds(0, 7)], st_send.at[0, 1]))
    pending.append((core == 1, g1_all.at[pl.ds(0, 8)], st_send.at[0, 1]))

    @pl.when(core == 0)
    def _():
        g1_all[region] = g1_in[...]

    hand_out(kown, kdist, kd_send, kd_recv)
    kdist[block] = kown[...]

    loads[6].wait()
    sums_of(emat, ecoef, share)
    coupling()

    for c, count in ((0, 7), (1, 8)):
        @pl.when(core == c)
        def _(count=count):
            finished(g1_all.at[pl.ds(0, count)], st_recv.at[0, 1])

    total = jnp.zeros((32, NRHS), f32)
    for i in range(8):
        at = 2 * i + lax.rem(region + core, 2)
        hi, lo = split(g1_all[at, :, 0, :])
        total = total + (dot(kpair[at], hi) + dot(kpair[at], lo))
    half_out[...] = add_up(total[16:])
    send(half_out, half_in, sib_send.at[1], sib_recv.at[1], sibling)
    pending.append((None, half_out, sib_send.at[1]))
    finished(half_in, sib_recv.at[1])
    a_out[0] = add_up(total[:16]) + half_in[...]
    swap_amplitudes(0, range(4))
    xbuf[...] = jnp.zeros_like(xbuf)
    amplitude_done(0, range(4))
    for j in range(SLOTS):
        value = spread_modes(mt[j], a_out[0] - al_all[0][facing[j]])
        lam[j] = value
        lower(j, value)

    def sum_start(out, arrived, k, stage):
        axis, me = (("block", block), ("region", region))[stage]
        all_to(
            axis, me, lambda to: out.at[stage], arrived.at[stage],
            st_send.at[k, stage], st_recv.at[k, stage],
        )
        arrived[stage, me] = out[stage]

    def sum_wait(out, arrived, k, stage):
        await_all(arrived.at[stage], st_recv.at[k, stage])
        out[stage + 1] = jnp.sum(arrived[stage], axis=0)

    def send_faces(k):
        for f in range(4):
            @pl.when(present[f])
            def _(f=f):
                send(
                    face_out.at[k - 1, f], face_in[k - 1].at[f ^ 1],
                    fc_send.at[k - 1, f], fc_recv.at[k - 1, f ^ 1], peer[f],
                )

            pending.append((present[f], face_out.at[k - 1, f], fc_send.at[k - 1, f]))

    def gather_send(k, coef, sign):
        both = dot(coef[...], low[...])
        mine = None
        for j in range(SLOTS):
            term = add_up(both[16 * j:16 * j + 16])
            if sign < 0:
                term = gcoef[j] - term
            pbuf[j] = term
            mine = term if mine is None else mine + term
        xbuf[rows8(block), :] = mine
        for f in range(4):
            term = pbuf[slot_ref[0, f]]

            @pl.when(present[f])
            def _(f=f, term=term):
                xbuf[rows8(place[f]), :] = -term
        s1_out[k] = xbuf[...].T.reshape(16, 8, 128)
        all_to(
            "block", block, lambda to: s1_out.at[k, to], s1_in.at[k],
            st_send.at[k, 0], st_recv.at[k, 0],
        )
        s1_in[k, block] = s1_out[k, block]

    def faces_send(k):
        for f in range(4):
            face_out[k - 1, f] = wloc[slot_ref[0, f]]
        send_faces(k)

    def gathered(k):
        await_all(s1_in.at[k], st_recv.at[k, 0])
        main = jnp.zeros((8, 128), f32)
        before = jnp.zeros((8, 128), f32)
        after = jnp.zeros((8, 128), f32)
        for t in range(NBK):
            tile = s1_in[k, t]
            main = main + jnp.where((lane_blk >= t - 1) & (lane_blk <= t + 1), tile, 0.0)
            before = before + jnp.where(lane_blk == (t + 8) % 16, tile, 0.0)
            after = after + jnp.where(lane_blk == (t + 9) % 16, tile, 0.0)
        return main, pltpu.roll(before, 64, 1), pltpu.roll(after, 56, 1)

    def regions_send(k, tiles):
        for i in range(3):
            s2_out[k, i] = tiles[i]
        all_to(
            "region", region, lambda to: s2_out.at[k], s2_in.at[k],
            st_send.at[k, 1], st_recv.at[k, 1],
        )
        s2_in[k, region] = s2_out[k]

    def solved(k):
        await_all(s2_in.at[k], st_recv.at[k, 1])
        pieces = []
        for r in range(NR):
            tile = s2_in[k, r, 0]
            if r < NR - 1:
                tile = tile + s2_in[k, r + 1, 1]
            if r > 0:
                tile = tile + s2_in[k, r - 1, 2]
            hi = tile.astype(bf16).astype(f32)
            pieces.append(jnp.concatenate([hi, tile - hi], axis=0).astype(bf16))
        left = jnp.concatenate(pieces, axis=1)
        both = dot(left, khi[...]) + dot(left, klo[...])
        s3_out[k] = both[:8] + both[8:]
        all_to(
            "block", block, lambda to: s3_out.at[k], s3_in.at[k],
            st_send.at[k, 2], st_recv.at[k, 2],
        )
        s3_in[k, block] = s3_out[k]

    def returned(k):
        await_all(s3_in.at[k], st_recv.at[k, 2])
        abuf[...] = s3_in[k].reshape(128, 128).T
        a_out[k] = abuf[rows8(block), :]
        swap_amplitudes(k, range(2))
        for f, near in ((2, block - 1), (3, block + 1)):
            @pl.when(present[f])
            def _(f=f, near=near):
                al_near[k][f - 2] = abuf[rows8(near), :]

    def faces_wait(k):
        for f in range(4):
            @pl.when(present[f])
            def _(f=f):
                pltpu.make_async_copy(
                    face_out.at[k - 1, f], face_in[k - 1].at[f], fc_recv.at[k - 1, f]
                ).wait()

    def whole(k, j):
        return wloc[j] + face_in[k - 1][facing[j]]

    def less_field(k, value_of):
        for j in range(SLOTS):
            near = spread_modes(mt[j], a_out[k] - al_near[k][beside[j]])
            part[j] = value_of(j) - near
        amplitude_done(k, range(2))
        for f in range(2):
            corr[f] = spread_modes(mt[slot_ref[0, f]], al_all[k][f])

    def assembled(j):
        return part[j] + corr[across[j]]

    def coarse_round(k, coef, sign, multiply, prepare):
        gather_send(k, coef, sign)
        multiply()
        faces_send(k)
        regions_send(k, gathered(k))
        prepare()
        solved(k)
        returned(k)
        faces_wait(k)
        less_field(k, lambda j: whole(k, j))

    def inner(total, left, right):
        return total + jnp.sum((left * right).reshape(FACE // 8, 8, NRHS), axis=0)

    def finish(total):
        return jnp.sum(total, axis=0, keepdims=True)

    zero8 = jnp.zeros((8, NRHS), f32)

    def coarse_matrix():
        finished(kdist.at[pl.ds(0, 7)], kd_recv.at[1])
        for r in range(NR):
            hi, lo = split(kdist[:, r].reshape(128, 128).T)
            khi[128 * r:128 * r + 128, :] = hi
            klo[128 * r:128 * r + 128, :] = lo

    def dual_start():
        for j in range(SLOTS):
            wloc[j] = gap_v[FACE * j:FACE * j + FACE, :] - product(dmat, j)
        hand_on(kdist, kd_send, kd_recv)

    def dirichlet():
        for j in range(SLOTS):
            wloc[j] = share[j] * product(emat, j)

    def unpacked(tile, b):
        before = jnp.where(lane_blk == (b + 8) % 16, tile, 0.0)
        after = jnp.where(lane_blk == (b + 9) % 16, tile, 0.0)
        return (
            jnp.where((lane_blk >= b - 1) & (lane_blk <= b + 1), tile, 0.0),
            pltpu.roll(before, 64, 1), pltpu.roll(after, 56, 1),
        )

    def coupling_matrix():
        finished(ldist.at[pl.ds(0, 7)], ld_recv.at[1])
        lmat[...] = jnp.zeros_like(lmat)
        for b in range(NBK):
            for g, at in enumerate((b + 16, b, b + 32, b + 15, b + 17)):
                if (g == 3 and b == 0) or (g == 4 and b == NBK - 1):
                    continue
                rows = slice(8 * at, 8 * at + 8)
                tile = ldist[b, g]
                for c, column in zip((128, 0, 256), unpacked(tile, b)):
                    lmat[rows, c:c + 128] = lmat[rows, c:c + 128] + column
        hi, lo = split(lmat[...])
        lhi[...] = hi
        llo[...] = lo

    def prepared():
        coupling_send()
        coarse_matrix()

    coarse_round(1, dcoef, -1, dual_start, prepared)
    for j in range(SLOTS):
        value = assembled(j)
        search[j] = value
        lower(j, share[j] * value)

    gather_send(2, ecoef, 1)
    dirichlet()
    faces_send(2)
    regions_send(2, gathered(2))
    faces_wait(2)
    for j in range(SLOTS):
        value = whole(2, j)
        direc[j] = value
        lower(j, value)
    gather_send(3, dcoef, 1)
    hand_on(ldist, ld_send, ld_recv)
    solved(2)
    for f in range(2):
        @pl.when(present[f])
        def _(f=f):
            send(s3_out.at[2], t_in.at[f ^ 1], t_send.at[f], t_recv.at[f ^ 1], peer[f])

        pending.append((present[f], s3_out.at[2], t_send.at[f]))
    coupling_matrix()
    tiles = gathered(3)
    for f in range(2):
        @pl.when(present[f])
        def _(f=f):
            finished(t_in.at[f], t_recv.at[f])
    pieces = []
    for tile in (t_in[0], s3_out[2], t_in[1]):
        hi = tile.astype(bf16).astype(f32)
        pieces.append(jnp.concatenate([hi, tile - hi], axis=0).astype(bf16))
    left = jnp.concatenate(pieces, axis=1)
    coupled = add_up(dot(left, lhi[...]) + dot(left, llo[...]))
    regions_send(
        3,
        (tiles[0] - coupled[:, 128:256], tiles[1] - coupled[:, 0:128], tiles[2] - coupled[:, 256:]),
    )
    returned(2)
    less_field(2, lambda j: direc[j])
    energy = zero8
    for j in range(SLOTS):
        value = assembled(j)
        direc[j] = value
        lower(j, value)
        energy = inner(energy, share[j] * search[j], value)
    curvature = zero8
    for j in range(SLOTS):
        value = product(dmat, j)
        wloc[j] = value
        field[j] = value
        curvature = inner(curvature, direc[j], value)
    c_out[0] = jnp.concatenate(
        [finish(energy), finish(curvature), jnp.zeros((6, NRHS), f32)], axis=0
    )
    sum_start(c_out, c_in, 6, 0)
    faces_send(3)
    solved(3)
    sum_wait(c_out, c_in, 6, 0)
    sum_start(c_out, c_in, 6, 1)
    returned(3)
    faces_wait(3)
    less_field(3, lambda j: whole(3, j))
    sum_wait(c_out, c_in, 6, 1)
    energy0 = c_out[2, 0:1, :]
    curvature0 = c_out[2, 1:2, :]
    step0 = energy0 / curvature0

    for j in range(SLOTS):
        value = search[j] - step0 * assembled(j)
        search[j] = value
        lower(j, share[j] * value)

    coarse_round(4, ecoef, 1, dirichlet, lambda: None)
    energy = zero8
    cross = zero8
    for j in range(SLOTS):
        value = assembled(j)
        lower(j, value)
        energy = inner(energy, share[j] * search[j], value)
        cross = inner(cross, value, field[j])
        search[j] = value
    curvature = zero8
    for j in range(SLOTS):
        curvature = inner(curvature, search[j], product(dmat, j))
    f_out[0] = jnp.concatenate(
        [finish(energy), finish(curvature), finish(cross), jnp.zeros((5, NRHS), f32)], axis=0
    )
    for stage in range(2):
        sum_start(f_out, f_in, 5, stage)
        sum_wait(f_out, f_in, 5, stage)
    energy1 = f_out[2, 0:1, :]
    beta = energy1 / energy0
    curvature1 = f_out[2, 1:2, :] + 2.0 * beta * f_out[2, 2:3, :] + beta * beta * curvature0
    step1 = energy1 / curvature1
    first = step0 + step1 * beta
    for j in range(SLOTS):
        out_ref[FACE * j:FACE * j + FACE, :] = lam[j] + first * direc[j] + step1 * search[j]

    for condition, ref, sem in pending:
        if condition is None:
            finished(ref, sem)
        else:
            @pl.when(condition)
            def _(ref=ref, sem=sem):
                finished(ref, sem)


def body(
    gap_terms, rigid_loads, dual_matrix, dirichlet_matrix, rigid_modes, coarse_rows,
    face_slot, glue_sign,
):
    vmem = pl.BlockSpec(memory_space=pltpu.VMEM)
    hbm = pl.BlockSpec(memory_space=pl.ANY)
    V = pltpu.VMEM
    slots = (SLOTS, FACE, NRHS)
    scratch = [
        V((6, 1, NRHS), f32), V((6, 1, NL), f32), V((6, 1, NL), f32), V((1, NL), jnp.int32),
        V((NL, NL), bf16), V((NL, NL), bf16), V((NL, NRHS), f32), V((NL, NRHS), f32),
        V((16, NL), bf16), V((16, NL), bf16), V((SLOTS, FACE, 32), bf16), V((2, 8, NL), f32),
        V((6, 1, NL), f32), V((NR, 32, 96), bf16), V((NR, 8, 128), f32), V((NBK, NR, 8, 128), f32),
        V((NR * 128, 128), bf16), V((NR * 128, 128), bf16),
        V((96, NL), bf16), V((96, NL), bf16), V((SLOTS, 8, NRHS), f32),
        V((128, 128), f32), V((5, 8, 128), f32), V((NBK, 5, 8, 128), f32),
        V((384, 384), f32), V((384, 384), bf16), V((384, 384), bf16), V((2, 8, 128), f32),
        V(slots, f32), V(slots, f32), V(slots, f32), V(slots, f32), V(slots, f32),
        V((NL, NRHS), bf16), V((SLOTS, 8, NRHS), f32), V((128, 128), f32), V((128, 128), f32),
        V((96, 1, 128), f32), V((NR, 96, 1, 128), f32), V((8, 128), f32), V((8, 128), f32),
        V((ROUNDS, NBK, 8, 128), f32), V((ROUNDS, NBK, 8, 128), f32),
        V((ROUNDS, 3, 8, 128), f32), V((ROUNDS, NR, 3, 8, 128), f32),
        V((ROUNDS, 8, 128), f32), V((ROUNDS, NBK, 8, 128), f32),
        V((ROUNDS, 8, 128), f32), tuple(V((5, 8, 128), f32) for _ in range(ROUNDS)),
        tuple(V((3, 8, 128), f32) for _ in range(ROUNDS)), V(slots, f32), V((3, FACE, NRHS), f32),
        V((4, 4, FACE, NRHS), f32), tuple(V((5, FACE, NRHS), f32) for _ in range(4)),
        V((3, 8, 128), f32), V((2, 16, 8, 128), f32),
        V((3, 8, 128), f32), V((2, 16, 8, 128), f32),
        pltpu.SemaphoreType.DMA((7,)), pltpu.SemaphoreType.DMA((2,)), pltpu.SemaphoreType.DMA((2,)),
        pltpu.SemaphoreType.DMA((2,)), pltpu.SemaphoreType.DMA((2,)),
        pltpu.SemaphoreType.DMA((2,)), pltpu.SemaphoreType.DMA((2,)),
        pltpu.SemaphoreType.DMA((2,)), pltpu.SemaphoreType.DMA((2,)),
        pltpu.SemaphoreType.DMA((ROUNDS + 2, 3)), pltpu.SemaphoreType.DMA((ROUNDS + 2, 3)),
        pltpu.SemaphoreType.DMA((ROUNDS, 4)), pltpu.SemaphoreType.DMA((ROUNDS, 4)),
        pltpu.SemaphoreType.DMA((4, 4)), pltpu.SemaphoreType.DMA((4, 4)),
    ]
    result = pl.pallas_call(
        kernel,
        out_shape=jax.ShapeDtypeStruct((NL, NRHS), f32),
        in_specs=[hbm] * 6 + [pl.BlockSpec(memory_space=pltpu.SMEM), hbm],
        out_specs=vmem,
        scratch_shapes=scratch,
        compiler_params=pltpu.CompilerParams(
            collective_id=0, has_side_effects=True, vmem_limit_bytes=60 * 1024 * 1024,
        ),
        cost_estimate=pl.CostEstimate(
            flops=5 * 2 * NL * NL * NRHS, bytes_accessed=12 * 1024 * 1024, transcendentals=0
        ),
    )(
        gap_terms, rigid_loads.transpose(0, 2, 1, 3), dual_matrix, dirichlet_matrix,
        rigid_modes.transpose(0, 2, 1, 3), coarse_rows.transpose(0, 2, 1, 3),
        face_slot, glue_sign,
    )
    return result[None, None]


def solution(mesh):
    matrix = P("region", "block", None, None)
    vector = P("region", "block", None)
    return jax.shard_map(
        body, mesh=mesh, in_specs=(matrix,) * 6 + (vector,) * 2, out_specs=matrix,
        check_vma=False,
    )
```

time: 147 us -> 114 us (0.78)
  Pallas kernels: 142 us -> 112 us
  local copies, waits for them, and re-layouts: 4.84 us -> 2.06 us
    pallas_call x1, Pallas kernels: 142 us -> 112 us  [body(): pl.pallas_call(kernel, out_shape=jax.ShapeDtypeStruct((NL, NRHS), f32), i...]
    unnamed x9 -> x1, local copies, waits for them, and re-layouts: 4.84 us -> 2.06 us
where the time goes in v2:
time: 114 us
  Pallas kernels  112 us (98%)
  local copies, waits for them, and re-layouts  2.06 us (2%)
    pallas_call x1, Pallas kernels, body(): pl.pallas_call(kernel, out_shape=jax.ShapeDtypeStruct((NL, NRHS), f32), i...  112 us

profile of v2, /device:TPU:1, one launch (start us, length us, event | category | flops | bytes accessed | tf_op | source)
XLA Modules:
  0.0 114.0 jit_solution(16325857376627280640)
XLA Ops:
  0.0 112.0 %shard_map.82 = f32[1536,128]{1,0:T(8,128)} custom-call(f32[1,1,1536,128]{3,2,1,0:T(8,128)} %gap_hbm.1, f32[1,6,1,128]{3,2,1,0:T(1,128)} %bitcast.7, bf16[1,1,1536,1536]{3,2,1,0:T(8,128)(2,1)} %dual_hbm.1, bf16[1,1,1536,1536]{3,2,1,0:T(8,128)(2,1)} %diri_hbm.1, f32[1,6,1,1536]{3,2,1,0:T(1,128)} %bitcast.5, f32[1,6,1,1536]{3,2,1,0:T(1,128)} %bitcast.6, ...), custom_call_target="tpu_custom_call" | custom-call | flops 3019898880 | bytes 12582912 | tf_op jit(solution)/shard_map/pallas_call | solution.py:670
  112.0 2.1 %copy.10 = f32[1,1,1536,128]{3,2,1,0:T(8,128)} copy(f32[1,1,1536,128]{3,2,1,0:T(8,128)} %bitcast.4) | data formatting | bytes 1572864

commit v3 on v2

--- a/solution.py
+++ b/solution.py
@@ -122,7 +122,8 @@
         @pl.when(jnp.logical_not(present[f]))
         def _(f=f):
             if f < 2:
-                t_in[f] = jnp.zeros((8, 128), f32)
+                for ref in t_in:
+                    ref[f] = jnp.zeros((8, 128), f32)
             for ref in al_all:
                 ref[f] = jnp.zeros((8, NRHS), f32)
             if f >= 2:
@@ -335,18 +336,6 @@
         lam[j] = value
         lower(j, value)
 
-    def sum_start(out, arrived, k, stage):
-        axis, me = (("block", block), ("region", region))[stage]
-        all_to(
-            axis, me, lambda to: out.at[stage], arrived.at[stage],
-            st_send.at[k, stage], st_recv.at[k, stage],
-        )
-        arrived[stage, me] = out[stage]
-
-    def sum_wait(out, arrived, k, stage):
-        await_all(arrived.at[stage], st_recv.at[k, stage])
-        out[stage + 1] = jnp.sum(arrived[stage], axis=0)
-
     def send_faces(k):
         for f in range(4):
             @pl.when(present[f])
@@ -358,9 +347,9 @@
 
             pending.append((present[f], face_out.at[k - 1, f], fc_send.at[k - 1, f]))
 
-    def gather_send(k, coef, sign):
+    def gather_send(k, coef, sign, extra=None, aside=None):
         both = dot(coef[...], low[...])
-        mine = None
+        mine = extra
         for j in range(SLOTS):
             term = add_up(both[16 * j:16 * j + 16])
             if sign < 0:
@@ -368,6 +357,8 @@
             pbuf[j] = term
             mine = term if mine is None else mine + term
         xbuf[rows8(block), :] = mine
+        if aside is not None:
+            xbuf[rows8(lax.rem(block + 4, 16)), :] = aside
         for f in range(4):
             term = pbuf[slot_ref[0, f]]
 
@@ -527,68 +518,133 @@
         search[j] = value
         lower(j, share[j] * value)
 
+    def owners_swap(i, k):
+        for f in range(2):
+            @pl.when(present[f])
+            def _(f=f):
+                send(
+                    s3_out.at[k], t_in[i].at[f ^ 1], t_send.at[i, f], t_recv.at[i, f ^ 1], peer[f]
+                )
+
+            pending.append((present[f], s3_out.at[k], t_send.at[i, f]))
+
+    def owners_coupled(i, k):
+        for f in range(2):
+            @pl.when(present[f])
+            def _(f=f):
+                finished(t_in[i].at[f], t_recv.at[i, f])
+        pieces = []
+        for tile in (t_in[i][0], s3_out[k], t_in[i][1]):
+            hi = tile.astype(bf16).astype(f32)
+            pieces.append(jnp.concatenate([hi, tile - hi], axis=0).astype(bf16))
+        left = jnp.concatenate(pieces, axis=1)
+        return add_up(dot(left, lhi[...]) + dot(left, llo[...]))
+
+    lane_mode = lane_8 & 7
+    six = jnp.zeros((6, NRHS), f32)
+
+    def in_modes(x):
+        return jnp.where(lane_mode < 6, x, 0.0)
+
+    def row_sum(x):
+        return jnp.sum(x, axis=1, keepdims=True)
+
+    def search_coefficients():
+        total = zero8
+        for j in range(SLOTS):
+            rows = slice(FACE * j, FACE * j + FACE)
+            hi, lo = split(search[j])
+            total = total + add_up(dot(m16[:, rows], hi) + dot(m16[:, rows], lo))
+        return total
+
+    def gather_with_sums(k, energy, cross, curvature, aside):
+        extra = jnp.concatenate([six, finish(energy), finish(cross)], axis=0)
+        one = jnp.zeros((1, NRHS), f32)
+        aside = aside + jnp.concatenate([six, finish(curvature), one], axis=0)
+        gather_send(k, dcoef, 1, extra, aside)
+
+    def column_sums(i, k, gather, tiles, coupled):
+        main, before, after = tiles
+        beyond = zero8
+        for t in range(NBK):
+            beyond = beyond + jnp.where(lane_blk == (t + 4) % 16, s1_in[gather, t], 0.0)
+        beyond = pltpu.roll(beyond, 96, 1)
+        own, prior, later = s3_out[k], t_in[i][0], t_in[i][1]
+        energy = row_sum(jnp.where(lane_mode == 6, main, 0.0) - in_modes(own * beyond))
+        curvature = row_sum(
+            jnp.where(lane_mode == 6, beyond, 0.0)
+            + in_modes(
+                own * (coupled[:, 128:256] - 2.0 * main)
+                + prior * (coupled[:, 0:128] - 2.0 * before)
+                + later * (coupled[:, 256:] - 2.0 * after)
+            )
+        )
+        return jnp.where(lane_8 == 0, energy, 0.0) + jnp.where(lane_8 == 1, curvature, 0.0)
+
+    def sums_start(out, arrived, k, stage):
+        axis, me = (("region", region), ("block", block))[stage]
+        all_to(
+            axis, me, lambda to: out.at[stage], arrived.at[stage],
+            st_send.at[k, stage], st_recv.at[k, stage],
+        )
+        arrived[stage, me] = out[stage]
+
+    def sums_pass(out, arrived, k):
+        await_all(arrived.at[0], st_recv.at[k, 0])
+        out[1] = jnp.sum(arrived[0], axis=0)
+        sums_start(out, arrived, k, 1)
+
+    def sums_here(arrived, k):
+        await_all(arrived.at[1], st_recv.at[k, 1])
+        return arrived[1].reshape(128, 128).T
+
     gather_send(2, ecoef, 1)
     dirichlet()
     faces_send(2)
+    aside = search_coefficients()
     regions_send(2, gathered(2))
     faces_wait(2)
+    energy = zero8
     for j in range(SLOTS):
         value = whole(2, j)
         direc[j] = value
         lower(j, value)
-    gather_send(3, dcoef, 1)
+        energy = inner(energy, share[j] * search[j], value)
+    curvature = zero8
+    for j in range(SLOTS):
+        curvature = inner(curvature, direc[j], product(dmat, j))
+    gather_with_sums(3, energy, zero8, curvature, aside)
     hand_on(ldist, ld_send, ld_recv)
     solved(2)
-    for f in range(2):
-        @pl.when(present[f])
-        def _(f=f):
-            send(s3_out.at[2], t_in.at[f ^ 1], t_send.at[f], t_recv.at[f ^ 1], peer[f])
-
-        pending.append((present[f], s3_out.at[2], t_send.at[f]))
+    owners_swap(0, 2)
     coupling_matrix()
     tiles = gathered(3)
-    for f in range(2):
-        @pl.when(present[f])
-        def _(f=f):
-            finished(t_in.at[f], t_recv.at[f])
-    pieces = []
-    for tile in (t_in[0], s3_out[2], t_in[1]):
-        hi = tile.astype(bf16).astype(f32)
-        pieces.append(jnp.concatenate([hi, tile - hi], axis=0).astype(bf16))
-    left = jnp.concatenate(pieces, axis=1)
-    coupled = add_up(dot(left, lhi[...]) + dot(left, llo[...]))
+    coupled = owners_coupled(0, 2)
     regions_send(
         3,
         (tiles[0] - coupled[:, 128:256], tiles[1] - coupled[:, 0:128], tiles[2] - coupled[:, 256:]),
     )
+    c_out[0] = column_sums(0, 2, 3, tiles, coupled)
+    sums_start(c_out, c_in, 6, 0)
     returned(2)
     less_field(2, lambda j: direc[j])
-    energy = zero8
     for j in range(SLOTS):
         value = assembled(j)
         direc[j] = value
         lower(j, value)
-        energy = inner(energy, share[j] * search[j], value)
-    curvature = zero8
     for j in range(SLOTS):
         value = product(dmat, j)
         wloc[j] = value
         field[j] = value
-        curvature = inner(curvature, direc[j], value)
-    c_out[0] = jnp.concatenate(
-        [finish(energy), finish(curvature), jnp.zeros((6, NRHS), f32)], axis=0
-    )
-    sum_start(c_out, c_in, 6, 0)
     faces_send(3)
     solved(3)
-    sum_wait(c_out, c_in, 6, 0)
-    sum_start(c_out, c_in, 6, 1)
+    sums_pass(c_out, c_in, 6)
     returned(3)
     faces_wait(3)
     less_field(3, lambda j: whole(3, j))
-    sum_wait(c_out, c_in, 6, 1)
-    energy0 = c_out[2, 0:1, :]
-    curvature0 = c_out[2, 1:2, :]
+    sums = sums_here(c_in, 6)
+    energy0 = sums[0:1, :]
+    curvature0 = sums[1:2, :]
     step0 = energy0 / curvature0
 
     for j in range(SLOTS):
@@ -596,27 +652,45 @@
         search[j] = value
         lower(j, share[j] * value)
 
-    coarse_round(4, ecoef, 1, dirichlet, lambda: None)
+    gather_send(4, ecoef, 1)
+    dirichlet()
+    faces_send(4)
+    aside = search_coefficients()
+    regions_send(4, gathered(4))
+    faces_wait(4)
     energy = zero8
     cross = zero8
     for j in range(SLOTS):
-        value = assembled(j)
+        value = whole(4, j)
+        wloc[j] = value
         lower(j, value)
         energy = inner(energy, share[j] * search[j], value)
         cross = inner(cross, value, field[j])
-        search[j] = value
     curvature = zero8
     for j in range(SLOTS):
-        curvature = inner(curvature, search[j], product(dmat, j))
-    f_out[0] = jnp.concatenate(
-        [finish(energy), finish(curvature), finish(cross), jnp.zeros((5, NRHS), f32)], axis=0
+        curvature = inner(curvature, wloc[j], product(dmat, j))
+    gather_with_sums(5, energy, cross, curvature, aside)
+    solved(4)
+    owners_swap(1, 4)
+    tiles = gathered(5)
+    coupled = owners_coupled(1, 4)
+    crossed = row_sum(
+        jnp.where(lane_mode == 7, tiles[0], 0.0)
+        - in_modes(
+            s3_out[4] * s2_out[3, 0] + t_in[1][0] * s2_out[3, 1] + t_in[1][1] * s2_out[3, 2]
+        )
     )
-    for stage in range(2):
-        sum_start(f_out, f_in, 5, stage)
-        sum_wait(f_out, f_in, 5, stage)
-    energy1 = f_out[2, 0:1, :]
+    f_out[0] = column_sums(1, 4, 5, tiles, coupled) + jnp.where(lane_8 == 2, crossed, 0.0)
+    sums_start(f_out, f_in, 7, 0)
+    returned(4)
+    less_field(4, lambda j: wloc[j])
+    for j in range(SLOTS):
+        search[j] = assembled(j)
+    sums_pass(f_out, f_in, 7)
+    sums = sums_here(f_in, 7)
+    energy1 = sums[0:1, :]
     beta = energy1 / energy0
-    curvature1 = f_out[2, 1:2, :] + 2.0 * beta * f_out[2, 2:3, :] + beta * beta * curvature0
+    curvature1 = sums[1:2, :] + 2.0 * beta * sums[2:3, :] + beta * beta * curvature0
     step1 = energy1 / curvature1
     first = step0 + step1 * beta
     for j in range(SLOTS):
@@ -647,11 +721,12 @@
         V((NR * 128, 128), bf16), V((NR * 128, 128), bf16),
         V((96, NL), bf16), V((96, NL), bf16), V((SLOTS, 8, NRHS), f32),
         V((128, 128), f32), V((5, 8, 128), f32), V((NBK, 5, 8, 128), f32),
-        V((384, 384), f32), V((384, 384), bf16), V((384, 384), bf16), V((2, 8, 128), f32),
+        V((384, 384), f32), V((384, 384), bf16), V((384, 384), bf16),
+        tuple(V((2, 8, 128), f32) for _ in range(2)),
         V(slots, f32), V(slots, f32), V(slots, f32), V(slots, f32), V(slots, f32),
         V((NL, NRHS), bf16), V((SLOTS, 8, NRHS), f32), V((128, 128), f32), V((128, 128), f32),
         V((96, 1, 128), f32), V((NR, 96, 1, 128), f32), V((8, 128), f32), V((8, 128), f32),
-        V((ROUNDS, NBK, 8, 128), f32), V((ROUNDS, NBK, 8, 128), f32),
+        V((ROUNDS + 1, NBK, 8, 128), f32), V((ROUNDS + 1, NBK, 8, 128), f32),
         V((ROUNDS, 3, 8, 128), f32), V((ROUNDS, NR, 3, 8, 128), f32),
         V((ROUNDS, 8, 128), f32), V((ROUNDS, NBK, 8, 128), f32),
         V((ROUNDS, 8, 128), f32), tuple(V((5, 8, 128), f32) for _ in range(ROUNDS)),
@@ -661,9 +736,9 @@
         V((3, 8, 128), f32), V((2, 16, 8, 128), f32),
         pltpu.SemaphoreType.DMA((7,)), pltpu.SemaphoreType.DMA((2,)), pltpu.SemaphoreType.DMA((2,)),
         pltpu.SemaphoreType.DMA((2,)), pltpu.SemaphoreType.DMA((2,)),
+        pltpu.SemaphoreType.DMA((2, 2)), pltpu.SemaphoreType.DMA((2, 2)),
         pltpu.SemaphoreType.DMA((2,)), pltpu.SemaphoreType.DMA((2,)),
-        pltpu.SemaphoreType.DMA((2,)), pltpu.SemaphoreType.DMA((2,)),
-        pltpu.SemaphoreType.DMA((ROUNDS + 2, 3)), pltpu.SemaphoreType.DMA((ROUNDS + 2, 3)),
+        pltpu.SemaphoreType.DMA((ROUNDS + 3, 3)), pltpu.SemaphoreType.DMA((ROUNDS + 3, 3)),
         pltpu.SemaphoreType.DMA((ROUNDS, 4)), pltpu.SemaphoreType.DMA((ROUNDS, 4)),
         pltpu.SemaphoreType.DMA((4, 4)), pltpu.SemaphoreType.DMA((4, 4)),
     ]

time: 114 us -> 109 us (0.956)
  Pallas kernels: 112 us -> 107 us
    pallas_call x1, Pallas kernels: 112 us -> 107 us  [body(): pl.pallas_call(kernel, out_shape=jax.ShapeDtypeStruct((NL, NRHS), f32), i...]
where the time goes in v3:
time: 109 us
  Pallas kernels  107 us (98%)
  local copies, waits for them, and re-layouts  2.06 us (2%)
    pallas_call x1, Pallas kernels, body(): pl.pallas_call(kernel, out_shape=jax.ShapeDtypeStruct((NL, NRHS), f32), i...  107 us

profile of v3, /device:TPU:1, one launch (start us, length us, event | category | flops | bytes accessed | tf_op | source)
XLA Modules:
  0.0 108.6 jit_solution(9457775686256325168)
XLA Ops:
  0.0 106.5 %shard_map.82 = f32[1536,128]{1,0:T(8,128)} custom-call(f32[1,1,1536,128]{3,2,1,0:T(8,128)} %gap_hbm.1, f32[1,6,1,128]{3,2,1,0:T(1,128)} %bitcast.7, bf16[1,1,1536,1536]{3,2,1,0:T(8,128)(2,1)} %dual_hbm.1, bf16[1,1,1536,1536]{3,2,1,0:T(8,128)(2,1)} %diri_hbm.1, f32[1,6,1,1536]{3,2,1,0:T(1,128)} %bitcast.5, f32[1,6,1,1536]{3,2,1,0:T(1,128)} %bitcast.6, ...), custom_call_target="tpu_custom_call" | custom-call | flops 3019898880 | bytes 12582912 | tf_op jit(solution)/shard_map/pallas_call | solution.py:745
  106.6 2.1 %copy.10 = f32[1,1,1536,128]{3,2,1,0:T(8,128)} copy(f32[1,1,1536,128]{3,2,1,0:T(8,128)} %bitcast.4) | data formatting | bytes 1572864
